TPU v7x, 32 devices: a whole 2x2x4 slice. The times are simulated.
32 devices in a mesh: groups: 2 (over y), rows: 2 (over x), expert: 4 (over z), pair: 2 (over core).
Axes of the slice: x: 2, y: 2, z: 4, core: 2. Of those that a mesh axis runs over, the one named last changes fastest.
Arguments:
- acts: bfloat16 [512, 6144], P(('groups', 'rows', 'expert'), 'pair'), parts along dimension 0, may hold values from -6 to 6
- grads: bfloat16 [512, 2, 16384], P(('groups', 'rows', 'expert'), None, 'pair'), parts along dimension 0, may hold values from -0.1796875 to 0.1796875
- routes: int32 [512, 2], P(('groups', 'rows', 'expert')), parts along dimension 0, may hold values from 0 to 3, all different within a row; in each aligned block of 32 rows (0 to 31, 32 to 63, ...) at most 24 rows name the same one
- seq_ids: int32 [512], P(('groups', 'rows', 'expert')), parts along dimension 0, may hold values from 0 to 3, never falling along the last dimension, each value on 1 to 96 neighbouring positions
- p_in: bfloat16 [4, 2, 3072, 64], P('expert', 'pair', 'rows'), may hold values from -0.078125 to 0.078125
- p_out: bfloat16 [4, 2, 8192, 64], P('expert', 'pair', 'rows'), may hold values from -0.046875 to 0.046875
Outputs:
- features: float32 [8, 4, 4096], P('groups', 'expert', ('rows', 'pair')), parts along dimension 0
There are 2 independent parts, one for each index of `groups`. A program takes and returns all parts, laid end to end along the dimension named above; an argument that names none is the same for every part. Nothing has to cross between parts.
Inputs may be any that keep to these rules, and one draw needn't show every extreme that they name: `routes`: in the rows of one device (aligned blocks of 32 tokens) no expert is named by more than 24 entries, and in every draw some expert is named by exactly 24 entries in some block; a token never names one expert twice. `seq_ids`: never falling along the tokens; every sequence holds 1 to 96 tokens, one exactly that many.
All inputs are finite; a program needn't handle non-finite values.
Results may differ from a plain program's by a relative error of at most 0.0003.
Values may be sent and summed in bfloat16 or wider, within the bound.
A program may use at most 64 MiB of HBM per device.

v0:
```python
import jax
import jax.numpy as jnp
from jax import lax
from jax.sharding import PartitionSpec as P

SEQS = 4


def bucket_entries(routes, n_experts, capacity):
    flat = routes.reshape(-1)
    expert_range = jnp.arange(n_experts, dtype=jnp.int32)
    member = (flat[:, None] == expert_range[None, :]).astype(jnp.int32)
    places = jnp.cumsum(member, axis=0) - 1
    place = jnp.sum(places * member, axis=1)
    slot_range = jnp.arange(capacity, dtype=jnp.int32)
    hits = member[:, :, None] * (place[:, None, None] == slot_range[None, None, :]).astype(
        jnp.int32
    )
    entry_index = jnp.arange(flat.shape[0], dtype=jnp.int32)
    source = jnp.sum(hits * entry_index[:, None, None], axis=0)
    filled = jnp.sum(hits, axis=0)
    return (source, filled)


def per_device(acts, grads, routes, seq_ids, p_in, p_out):
    tok = routes.shape[0]
    top = routes.shape[1]
    half_d = acts.shape[1]
    half_ff = grads.shape[2]
    k_in = p_in.shape[3]
    k_out = p_out.shape[3]
    feat = k_in * k_out
    n_rows = lax.axis_size("rows")
    n_exp = lax.axis_size("expert") * p_in.shape[0]
    capacity = min(tok, 3 * tok // lax.axis_size("expert"))
    d_piece = half_d // n_rows
    f_piece = half_ff // n_rows
    seq_range = jnp.arange(SEQS, dtype=jnp.int32)
    source, filled = bucket_entries(routes, n_exp, capacity)
    token_of = source // top
    keep = filled.astype(jnp.bfloat16)[:, :, None]
    a_buckets = jnp.take(acts, token_of.reshape(-1), axis=0).reshape(n_exp, capacity, half_d) * keep
    g_buckets = (
        jnp.take(grads.reshape(tok * top, half_ff), source.reshape(-1), axis=0).reshape(
            n_exp, capacity, half_ff
        )
        * keep
    )
    labels = jnp.where(
        filled == 1, jnp.take(seq_ids, token_of.reshape(-1)).reshape(n_exp, capacity), -1
    )
    a_parts = a_buckets.reshape(n_exp, capacity, n_rows, d_piece).transpose(2, 0, 1, 3)
    g_parts = g_buckets.reshape(n_exp, capacity, n_rows, f_piece).transpose(2, 0, 1, 3)
    label_parts = jnp.broadcast_to(labels.astype(jnp.bfloat16)[None], (n_rows, n_exp, capacity))
    a_recv, g_recv, label_recv = (
        lax.all_to_all(
            a_parts.reshape(n_rows * n_exp, capacity, d_piece),
            ("rows", "expert"),
            split_axis=0,
            concat_axis=0,
            tiled=True,
        ),
        lax.all_to_all(
            g_parts.reshape(n_rows * n_exp, capacity, f_piece),
            ("rows", "expert"),
            split_axis=0,
            concat_axis=0,
            tiled=True,
        ),
        lax.all_to_all(
            label_parts.reshape(n_rows * n_exp, capacity),
            ("rows", "expert"),
            split_axis=0,
            concat_axis=0,
            tiled=True,
        ),
    )
    slots = n_rows * n_exp * capacity
    a_rows = a_recv.reshape(slots, d_piece)
    g_rows = g_recv.reshape(slots, f_piece)
    slot_labels = label_recv.reshape(slots).astype(jnp.int32)
    u_part = jnp.dot(a_rows, p_in.reshape(d_piece, k_in), preferred_element_type=jnp.float32)
    v_part = jnp.dot(g_rows, p_out.reshape(f_piece, k_out), preferred_element_type=jnp.float32)
    groups = lax.axis_size(("rows", "pair"))
    share = feat // groups
    u_all, v_all = lax.psum((u_part, v_part), ("rows", "pair"))
    columns = lax.axis_index(("rows", "pair")) * share + jnp.arange(share, dtype=jnp.int32)
    u_cols = jnp.take(u_all, columns // k_out, axis=1)
    v_cols = jnp.take(v_all, columns % k_out, axis=1)
    onehot = (slot_labels[None, :] == seq_range[:, None]).astype(jnp.float32)
    block = jnp.dot(onehot, u_cols * v_cols, precision=lax.Precision.HIGHEST)
    return block.reshape(SEQS, 1, share)


def solution(mesh):
    return jax.shard_map(
        per_device,
        mesh=mesh,
        in_specs=(
            P(("groups", "rows", "expert"), "pair"),
            P(("groups", "rows", "expert"), None, "pair"),
            P(("groups", "rows", "expert"), None),
            P(("groups", "rows", "expert")),
            P("expert", "pair", "rows", None),
            P("expert", "pair", "rows", None),
        ),
        out_specs=P("groups", "expert", ("rows", "pair")),
        check_vma=False,
    )
```

profile of v0, /device:TPU:0, one launch (start us, length us, event | category | flops | bytes accessed | tf_op | source)
XLA Modules:
  0.0 132.2 jit_solution(3614667889216256828)
XLA Ops:
  6.5 0.8 copy.22
  7.4 0.1 eq.62
  7.5 0.1 fusion.13
  7.5 0.1 copy.23
  7.6 0.1 reduce_window_sum.11
  7.7 0.2 select_reduce_fusion
  7.9 0.2 multiply_reduce_fusion
  8.1 0.1 reduce_sum.32
  8.3 1.6 %gather_fusion = s32[96]{0:T(128)S(1)} fusion(s32[32]{0:T(128)} %param.11, s32[1024]{0:T(1024)S(1)} %get-tuple-element.16), kind=kCustom, calls=%fused_computation.2 | custom fusion | bytes 1152 | tf_op jit(solution)/shard_map/jit(_take)/gather | solution.py:50
  9.9 0.1 gather.22
  9.9 0.9 gather_fusion.1
  10.9 0.4 gather.24
  11.3 1.0 fusion.4
  12.3 7.3 %all-to-all-start.1 = ((bf16[8,24,1536]{2,1,0:T(8,128)(2,1)}), bf16[8,24,1536]{2,1,0:T(8,128)(2,1)S(1)}, u32[]{:S(2)}, u32[]{:S(2)}) async-start(bf16[8,24,1536]{2,1,0:T(8,128)(2,1)} %bitcast.3), calls=%async_computation.1 | async-start | bytes 1179648 | tf_op jit(solution)/shard_map/all_to_all | solution.py:56
  19.6 0.4 reshape.266
  20.0 2.7 %gather_fusion.2 = bf16[96,8192]{1,0:T(8,128)(2,1)} fusion(bf16[64,8192]{1,0:T(8,128)(2,1)S(1)} %reshape.266, s32[1024]{0:T(1024)S(1)} %get-tuple-element.15), kind=kCustom, calls=%fused_computation.4 | custom fusion | bytes 3146112 | tf_op jit(solution)/shard_map/jit(_take)/gather | solution.py:44
  22.7 2.9 %gather.26 = bf16[4,24,2,4096]{3,2,1,0:T(2,128)(2,1)S(1)} reshape(bf16[96,8192]{1,0:T(8,128)(2,1)} %gather_fusion.2) | data formatting | bytes 3145728 | tf_op jit(solution)/shard_map/jit(_take)/gather | solution.py:44
  25.6 3.0 %fusion = bf16[4,24,2,4096]{3,1,0,2:T(8,128)(2,1)} fusion(bf16[4,24,2,4096]{3,2,1,0:T(2,128)(2,1)S(1)} %gather.26, pred[4,24]{1,0:T(4,128)(4,1)S(1)} %compare_and_fusion.2, bf16[4,24]{1,0:T(4,128)(2,1)S(1)} %get-tuple-element.12), kind=kLoop, calls=%fused_computation.6 | loop fusion | flops 1572864 | bytes 3146016 | tf_op jit(solution)/shard_map/mul | solution.py:44
  28.6 7.8 %all-to-all-done.1 = bf16[8,24,1536]{2,1,0:T(8,128)(2,1)S(1)} async-done(((bf16[8,24,1536]{2,1,0:T(8,128)(2,1)}), bf16[8,24,1536]{2,1,0:T(8,128)(2,1)S(1)}, u32[]{:S(2)}, u32[]{:S(2)}) %all-to-all-start.1) | async-done | bytes 589856 | tf_op jit(solution)/shard_map/all_to_all | solution.py:56
  36.3 3.7 %all-to-all-start.2 = ((bf16[8,24,4096]{2,1,0:T(8,128)(2,1)}), bf16[8,24,4096]{2,1,0:T(8,128)(2,1)S(1)}, u32[]{:S(2)}, u32[]{:S(2)}) async-start(bf16[8,24,4096]{2,1,0:T(8,128)(2,1)} %bitcast.32), calls=%async_computation.2 | async-start | bytes 3145728 | tf_op jit(solution)/shard_map/all_to_all | solution.py:63
  40.1 0.6 copy.24
  40.7 0.9 fusion.10
  41.6 35.0 %all-to-all-done.2 = bf16[8,24,4096]{2,1,0:T(8,128)(2,1)S(1)} async-done(((bf16[8,24,4096]{2,1,0:T(8,128)(2,1)}), bf16[8,24,4096]{2,1,0:T(8,128)(2,1)S(1)}, u32[]{:S(2)}, u32[]{:S(2)}) %all-to-all-start.2) | async-done | bytes 1572896 | tf_op jit(solution)/shard_map/all_to_all | solution.py:63
  76.6 3.3 %all-to-all-start = ((bf16[8,1,24]{2,1,0:T(2,128)(2,1)}), bf16[8,1,24]{2,1,0:T(2,128)(2,1)S(1)}, u32[]{:S(2)}, u32[]{:S(2)}) async-start(bf16[8,1,24]{2,1,0:T(2,128)(2,1)} %copy.24), calls=%async_computation | async-start | bytes 8192 | tf_op jit(solution)/shard_map/all_to_all | solution.py:70
  80.0 1.3 fusion.5
  81.3 5.0 %all-to-all-done = bf16[8,1,24]{2,1,0:T(2,128)(2,1)S(1)} async-done(((bf16[8,1,24]{2,1,0:T(2,128)(2,1)}), bf16[8,1,24]{2,1,0:T(2,128)(2,1)S(1)}, u32[]{:S(2)}, u32[]{:S(2)}) %all-to-all-start) | async-done | bytes 416 | tf_op jit(solution)/shard_map/all_to_all | solution.py:70
  86.3 0.1 reshape.271
  86.4 29.7 %all-reduce.3.cloned.1.call-done = (f32[192,64]{0,1:T(8,128)}, f32[192,64]{0,1:T(8,128)}) async-done(((f32[192,64]{0,1:T(8,128)}, f32[192,64]{0,1:T(8,128)}), (f32[192,64]{0,1:T(8,128)}, f32[192,64]{0,1:T(8,128)})) %all-reduce.3.cloned.1.call-update) | async-done | bytes 98320 | tf_op jit(solution)/shard_map/psum | solution.py:86
  116.1 4.3 %gather_fusion.4 = f32[1024,192]{1,0:T(8,128)S(1)} fusion(f32[192,64]{0,1:T(8,128)} %get-tuple-element.8, s32[1024]{0:T(1024)S(1)} %get-tuple-element.19), kind=kCustom, calls=%fused_computation.1.clone | custom fusion | bytes 1576960 | tf_op jit(solution)/shard_map/jit(_take)/gather | solution.py:89
  120.4 3.5 %gather_fusion.3 = f32[1024,192]{1,0:T(8,128)S(1)} fusion(f32[192,64]{0,1:T(8,128)S(1)} %copy-done.1, s32[1024]{0:T(1024)S(1)} %get-tuple-element.20), kind=kCustom, calls=%fused_computation.clone | custom fusion | bytes 1576960 | tf_op jit(solution)/shard_map/jit(_take)/gather | solution.py:88
  123.9 0.8 convolution_bitcast_fusion
  124.7 0.6 copy.27
  (21 shorter events, 0.2 us)
Async XLA Ops:
  6.5 73.5 %copy-start = (bf16[1,1,4096,64]{2,3,1,0:T(8,128)(2,1)S(1)}, bf16[1,1,4096,64]{2,3,1,0:T(8,128)(2,1)}, u32[]{:S(2)}) copy-start(bf16[1,1,4096,64]{2,3,1,0:T(8,128)(2,1)} %param.13) | copy-start | bytes 1572868
  6.5 3.4 %copy-start.2 = (bf16[32,3072]{1,0:T(8,128)(2,1)S(1)}, bf16[32,3072]{1,0:T(8,128)(2,1)}, u32[]{:S(2)}) copy-start(bf16[32,3072]{1,0:T(8,128)(2,1)} %param.8) | copy-start | bytes 589828
  10.9 8.7 %copy-start.3 = (bf16[32,2,8192]{2,1,0:T(2,128)(2,1)S(1)}, bf16[32,2,8192]{2,1,0:T(2,128)(2,1)}, u32[]{:S(2)}) copy-start(bf16[32,2,8192]{2,1,0:T(2,128)(2,1)} %param.9) | copy-start | bytes 3145732
  12.3 24.0 %all-to-all-start.1 = ((bf16[8,24,1536]{2,1,0:T(8,128)(2,1)}), bf16[8,24,1536]{2,1,0:T(8,128)(2,1)S(1)}, u32[]{:S(2)}, u32[]{:S(2)}) async-start(bf16[8,24,1536]{2,1,0:T(8,128)(2,1)} %bitcast.3), calls=%async_computation.1 | async-start | bytes 1179648 | tf_op jit(solution)/shard_map/all_to_all | solution.py:56
  36.3 4.4 %copy-start.4 = (bf16[1,1,1536,64]{2,3,1,0:T(8,128)(2,1)S(1)}, bf16[1,1,1536,64]{2,3,1,0:T(8,128)(2,1)}, u32[]{:S(2)}) copy-start(bf16[1,1,1536,64]{2,3,1,0:T(8,128)(2,1)} %param.12) | copy-start | bytes 589828
  36.3 40.3 %all-to-all-start.2 = ((bf16[8,24,4096]{2,1,0:T(8,128)(2,1)}), bf16[8,24,4096]{2,1,0:T(8,128)(2,1)S(1)}, u32[]{:S(2)}, u32[]{:S(2)}) async-start(bf16[8,24,4096]{2,1,0:T(8,128)(2,1)} %bitcast.32), calls=%async_computation.2 | async-start | bytes 3145728 | tf_op jit(solution)/shard_map/all_to_all | solution.py:63
  76.6 9.6 %all-to-all-start = ((bf16[8,1,24]{2,1,0:T(2,128)(2,1)}), bf16[8,1,24]{2,1,0:T(2,128)(2,1)S(1)}, u32[]{:S(2)}, u32[]{:S(2)}) async-start(bf16[8,1,24]{2,1,0:T(2,128)(2,1)} %copy.24), calls=%async_computation | async-start | bytes 8192 | tf_op jit(solution)/shard_map/all_to_all | solution.py:70
  80.0 36.1 %all-reduce.3.cloned.1.call-start = ((), (), s32[]{:S(2)}) async-start(), calls=%async_computation.3 | async-start | bytes 262144 | tf_op jit(solution)/shard_map/psum | solution.py:86
  116.1 4.3 %copy-start.1 = (f32[192,64]{0,1:T(8,128)S(1)}, f32[192,64]{0,1:T(8,128)}, u32[]{:S(2)}) copy-start(f32[192,64]{0,1:T(8,128)} %get-tuple-element.9) | copy-start | bytes 147460
Sparse Core Ops, SparseCore 0:
  83.2 32.8 all-reduce.2
where the time goes:
time: 133 us; the launch traced here: 132 us
  waiting for transfers between devices  77.4 us (58%)
  local copies, waits for them, and re-layouts  19.2 us (14%)
  starting transfers between devices  14.3 us (11%)
  between operations  13.6 us (10%)
  other arithmetic  4.63 us (3%)
  matrix products  2.98 us (2%)
    all_to_all x1, waiting for transfers between devices, per_device(): lax.all_to_all(g_parts.reshape(n_rows * n_exp, capacity, f_piece), ('rows...  35 us
    psum x1, waiting for transfers between devices, per_device(): u_all, v_all = lax.psum((u_part, v_part), ('rows', 'pair'))  29.7 us
    all_to_all x1, waiting for transfers between devices, per_device(): lax.all_to_all(a_parts.reshape(n_rows * n_exp, capacity, d_piece), ('rows...  7.76 us
    all_to_all x1, starting transfers between devices, per_device(): lax.all_to_all(a_parts.reshape(n_rows * n_exp, capacity, d_piece), ('rows...  7.25 us
    gather x2, local copies, waits for them, and re-layouts, per_device(): jnp.take(grads.reshape(tok * top, half_ff), source.reshape(-1), axis=0)  5.56 us
    all_to_all x1, waiting for transfers between devices, per_device(): lax.all_to_all(label_parts.reshape(n_rows * n_exp, capacity), ('rows', 'e...  4.98 us
    gather x1, local copies, waits for them, and re-layouts, per_device(): v_cols = jnp.take(v_all, columns % k_out, axis=1)  4.33 us
    all_to_all x1, starting transfers between devices, per_device(): lax.all_to_all(g_parts.reshape(n_rows * n_exp, capacity, f_piece), ('rows...  3.71 us
  transfers between devices with their start and end apart: 4, of which 4 were waited for; matrix products, arithmetic and copies ran while one was open for 9% of the time, Pallas kernels for 0%

commit v1 on v0

--- a/solution.py
+++ b/solution.py
@@ -83,7 +83,7 @@
     v_part = jnp.dot(g_rows, p_out.reshape(f_piece, k_out), preferred_element_type=jnp.float32)
     groups = lax.axis_size(("rows", "pair"))
     share = feat // groups
-    u_all, v_all = lax.psum((u_part, v_part), ("rows", "pair"))
+    u_all, v_all = lax.psum(lax.psum((u_part, v_part), "pair"), "rows")
     columns = lax.axis_index(("rows", "pair")) * share + jnp.arange(share, dtype=jnp.int32)
     u_cols = jnp.take(u_all, columns // k_out, axis=1)
     v_cols = jnp.take(v_all, columns % k_out, axis=1)

time: 133 us -> 144 us (1.083)
  waiting for transfers between devices: 77.4 us -> 88.9 us
    psum x1 -> x2, waiting for transfers between devices: 29.7 us -> 46.1 us  [per_device(): u_all, v_all = lax.psum(lax.psum((u_part, v_part), 'pair'), 'rows')]
    all_to_all x1, waiting for transfers between devices: 4.98 us -> 0.01 us  [per_device(): lax.all_to_all(label_parts.reshape(n_rows * n_exp, capacity), ('rows', 'e...]
  transfers between devices with their start and end apart: 4 -> 5, of which waited for: 4 -> 4; matrix products, arithmetic and copies ran while one was open for 9% -> 8% of each run, Pallas kernels for 0% -> 0%
where the time goes in v1:
time: 144 us
  waiting for transfers between devices  88.9 us (62%)
  local copies, waits for them, and re-layouts  19.2 us (13%)
  starting transfers between devices  14.4 us (10%)
  between operations  13.6 us (9%)
  other arithmetic  4.63 us (3%)
  matrix products  2.98 us (2%)
    psum x2, waiting for transfers between devices, per_device(): u_all, v_all = lax.psum(lax.psum((u_part, v_part), 'pair'), 'rows')  46.1 us
    all_to_all x1, waiting for transfers between devices, per_device(): lax.all_to_all(g_parts.reshape(n_rows * n_exp, capacity, f_piece), ('rows...  35 us
    all_to_all x1, waiting for transfers between devices, per_device(): lax.all_to_all(a_parts.reshape(n_rows * n_exp, capacity, d_piece), ('rows...  7.78 us
    all_to_all x1, starting transfers between devices, per_device(): lax.all_to_all(a_parts.reshape(n_rows * n_exp, capacity, d_piece), ('rows...  7.25 us
    gather x2, local copies, waits for them, and re-layouts, per_device(): jnp.take(grads.reshape(tok * top, half_ff), source.reshape(-1), axis=0)  5.55 us
    gather x1, local copies, waits for them, and re-layouts, per_device(): v_cols = jnp.take(v_all, columns % k_out, axis=1)  4.33 us
    all_to_all x1, starting transfers between devices, per_device(): lax.all_to_all(g_parts.reshape(n_rows * n_exp, capacity, f_piece), ('rows...  3.71 us
    gather x1, local copies, waits for them, and re-layouts, per_device(): u_cols = jnp.take(u_all, columns // k_out, axis=1)  3.47 us
  transfers between devices with their start and end apart: 5, of which 4 were waited for; matrix products, arithmetic and copies ran while one was open for 8% of the time, Pallas kernels for 0%

profile of v1, /device:TPU:0, one launch (start us, length us, event | category | flops | bytes accessed | tf_op | source)
XLA Modules:
  0.0 143.7 jit_solution(12240648069070171379)
XLA Ops:
  6.5 0.8 copy.22
  7.4 0.1 eq.62
  7.5 0.1 fusion.13
  7.5 0.1 copy.23
  7.6 0.1 reduce_window_sum.11
  7.7 0.2 select_reduce_fusion
  7.9 0.2 multiply_reduce_fusion
  8.1 0.1 reduce_sum.32
  8.3 1.6 %gather_fusion = s32[96]{0:T(128)S(1)} fusion(s32[32]{0:T(128)} %param.11, s32[1024]{0:T(1024)S(1)} %get-tuple-element.18), kind=kCustom, calls=%fused_computation.2 | custom fusion | bytes 1152 | tf_op jit(solution)/shard_map/jit(_take)/gather | solution.py:50
  9.9 0.1 gather.22
  9.9 0.9 gather_fusion.1
  10.9 0.4 gather.24
  11.3 1.0 fusion.4
  12.3 7.3 %all-to-all-start.1 = ((bf16[8,24,1536]{2,1,0:T(8,128)(2,1)}), bf16[8,24,1536]{2,1,0:T(8,128)(2,1)S(1)}, u32[]{:S(2)}, u32[]{:S(2)}) async-start(bf16[8,24,1536]{2,1,0:T(8,128)(2,1)} %bitcast.3), calls=%async_computation.1 | async-start | bytes 1179648 | tf_op jit(solution)/shard_map/all_to_all | solution.py:56
  19.6 0.4 reshape.266
  20.0 2.7 %gather_fusion.2 = bf16[96,8192]{1,0:T(8,128)(2,1)} fusion(bf16[64,8192]{1,0:T(8,128)(2,1)S(1)} %reshape.266, s32[1024]{0:T(1024)S(1)} %get-tuple-element.17), kind=kCustom, calls=%fused_computation.4 | custom fusion | bytes 3146112 | tf_op jit(solution)/shard_map/jit(_take)/gather | solution.py:44
  22.7 2.9 %gather.26 = bf16[4,24,2,4096]{3,2,1,0:T(2,128)(2,1)S(1)} reshape(bf16[96,8192]{1,0:T(8,128)(2,1)} %gather_fusion.2) | data formatting | bytes 3145728 | tf_op jit(solution)/shard_map/jit(_take)/gather | solution.py:44
  25.6 3.0 %fusion = bf16[4,24,2,4096]{3,1,0,2:T(8,128)(2,1)} fusion(bf16[4,24,2,4096]{3,2,1,0:T(2,128)(2,1)S(1)} %gather.26, pred[4,24]{1,0:T(4,128)(4,1)S(1)} %compare_and_fusion.2, bf16[4,24]{1,0:T(4,128)(2,1)S(1)} %get-tuple-element.14), kind=kLoop, calls=%fused_computation.6 | loop fusion | flops 1572864 | bytes 3146016 | tf_op jit(solution)/shard_map/mul | solution.py:44
  28.6 7.8 %all-to-all-done.1 = bf16[8,24,1536]{2,1,0:T(8,128)(2,1)S(1)} async-done(((bf16[8,24,1536]{2,1,0:T(8,128)(2,1)}), bf16[8,24,1536]{2,1,0:T(8,128)(2,1)S(1)}, u32[]{:S(2)}, u32[]{:S(2)}) %all-to-all-start.1) | async-done | bytes 589856 | tf_op jit(solution)/shard_map/all_to_all | solution.py:56
  36.3 3.7 %all-to-all-start.2 = ((bf16[8,24,4096]{2,1,0:T(8,128)(2,1)}), bf16[8,24,4096]{2,1,0:T(8,128)(2,1)S(1)}, u32[]{:S(2)}, u32[]{:S(2)}) async-start(bf16[8,24,4096]{2,1,0:T(8,128)(2,1)} %bitcast.32), calls=%async_computation.2 | async-start | bytes 3145728 | tf_op jit(solution)/shard_map/all_to_all | solution.py:63
  40.1 0.6 copy.24
  40.7 0.9 fusion.10
  41.6 35.0 %all-to-all-done.2 = bf16[8,24,4096]{2,1,0:T(8,128)(2,1)S(1)} async-done(((bf16[8,24,4096]{2,1,0:T(8,128)(2,1)}), bf16[8,24,4096]{2,1,0:T(8,128)(2,1)S(1)}, u32[]{:S(2)}, u32[]{:S(2)}) %all-to-all-start.2) | async-done | bytes 1572896 | tf_op jit(solution)/shard_map/all_to_all | solution.py:63
  76.6 3.3 %all-to-all-start = ((bf16[8,1,24]{2,1,0:T(2,128)(2,1)}), bf16[8,1,24]{2,1,0:T(2,128)(2,1)S(1)}, u32[]{:S(2)}, u32[]{:S(2)}) async-start(bf16[8,1,24]{2,1,0:T(2,128)(2,1)} %copy.24), calls=%async_computation | async-start | bytes 8192 | tf_op jit(solution)/shard_map/all_to_all | solution.py:70
  80.0 1.2 fusion.5
  81.4 21.2 %all-reduce.5.cloned.1.call-done = (f32[192,64]{0,1:T(8,128)}, f32[192,64]{0,1:T(8,128)}) async-done(((f32[192,64]{0,1:T(8,128)}, f32[192,64]{0,1:T(8,128)}), (f32[192,64]{0,1:T(8,128)}, f32[192,64]{0,1:T(8,128)})) %all-reduce.5.cloned.1.call-update) | async-done | bytes 98320 | tf_op jit(solution)/shard_map/psum | solution.py:86
  102.6 0.1 reshape.271
  102.7 25.0 %all-reduce.7.cloned.1.call-done = (f32[192,64]{0,1:T(8,128)}, f32[192,64]{0,1:T(8,128)}) async-done(((f32[192,64]{0,1:T(8,128)}, f32[192,64]{0,1:T(8,128)}), (f32[192,64]{0,1:T(8,128)}, f32[192,64]{0,1:T(8,128)})) %all-reduce.7.cloned.1.call-update) | async-done | bytes 98320 | tf_op jit(solution)/shard_map/psum | solution.py:86
  127.6 4.3 %gather_fusion.4 = f32[1024,192]{1,0:T(8,128)S(1)} fusion(f32[192,64]{0,1:T(8,128)} %get-tuple-element.10, s32[1024]{0:T(1024)S(1)} %get-tuple-element.21), kind=kCustom, calls=%fused_computation.1.clone | custom fusion | bytes 1576960 | tf_op jit(solution)/shard_map/jit(_take)/gather | solution.py:89
  132.0 3.5 %gather_fusion.3 = f32[1024,192]{1,0:T(8,128)S(1)} fusion(f32[192,64]{0,1:T(8,128)S(1)} %copy-done.1, s32[1024]{0:T(1024)S(1)} %get-tuple-element.22), kind=kCustom, calls=%fused_computation.clone | custom fusion | bytes 1576960 | tf_op jit(solution)/shard_map/jit(_take)/gather | solution.py:88
  135.4 0.8 convolution_bitcast_fusion
  136.2 0.6 copy.27
  (24 shorter events, 0.2 us)
Async XLA Ops:
  6.5 73.5 %copy-start = (bf16[1,1,4096,64]{2,3,1,0:T(8,128)(2,1)S(1)}, bf16[1,1,4096,64]{2,3,1,0:T(8,128)(2,1)}, u32[]{:S(2)}) copy-start(bf16[1,1,4096,64]{2,3,1,0:T(8,128)(2,1)} %param.13) | copy-start | bytes 1572868
  6.5 3.4 %copy-start.2 = (bf16[32,3072]{1,0:T(8,128)(2,1)S(1)}, bf16[32,3072]{1,0:T(8,128)(2,1)}, u32[]{:S(2)}) copy-start(bf16[32,3072]{1,0:T(8,128)(2,1)} %param.8) | copy-start | bytes 589828
  10.9 8.7 %copy-start.3 = (bf16[32,2,8192]{2,1,0:T(2,128)(2,1)S(1)}, bf16[32,2,8192]{2,1,0:T(2,128)(2,1)}, u32[]{:S(2)}) copy-start(bf16[32,2,8192]{2,1,0:T(2,128)(2,1)} %param.9) | copy-start | bytes 3145732
  12.3 24.0 %all-to-all-start.1 = ((bf16[8,24,1536]{2,1,0:T(8,128)(2,1)}), bf16[8,24,1536]{2,1,0:T(8,128)(2,1)S(1)}, u32[]{:S(2)}, u32[]{:S(2)}) async-start(bf16[8,24,1536]{2,1,0:T(8,128)(2,1)} %bitcast.3), calls=%async_computation.1 | async-start | bytes 1179648 | tf_op jit(solution)/shard_map/all_to_all | solution.py:56
  36.3 4.4 %copy-start.4 = (bf16[1,1,1536,64]{2,3,1,0:T(8,128)(2,1)S(1)}, bf16[1,1,1536,64]{2,3,1,0:T(8,128)(2,1)}, u32[]{:S(2)}) copy-start(bf16[1,1,1536,64]{2,3,1,0:T(8,128)(2,1)} %param.12) | copy-start | bytes 589828
  36.3 40.3 %all-to-all-start.2 = ((bf16[8,24,4096]{2,1,0:T(8,128)(2,1)}), bf16[8,24,4096]{2,1,0:T(8,128)(2,1)S(1)}, u32[]{:S(2)}, u32[]{:S(2)}) async-start(bf16[8,24,4096]{2,1,0:T(8,128)(2,1)} %bitcast.32), calls=%async_computation.2 | async-start | bytes 3145728 | tf_op jit(solution)/shard_map/all_to_all | solution.py:63
  76.6 25.9 %all-to-all-start = ((bf16[8,1,24]{2,1,0:T(2,128)(2,1)}), bf16[8,1,24]{2,1,0:T(2,128)(2,1)S(1)}, u32[]{:S(2)}, u32[]{:S(2)}) async-start(bf16[8,1,24]{2,1,0:T(2,128)(2,1)} %copy.24), calls=%async_computation | async-start | bytes 8192 | tf_op jit(solution)/shard_map/all_to_all | solution.py:70
  80.0 22.6 %all-reduce.5.cloned.1.call-start = ((), (), s32[]{:S(2)}) async-start(), calls=%async_computation.3 | async-start | bytes 262144 | tf_op jit(solution)/shard_map/psum | solution.py:86
  81.3 46.3 %all-reduce.7.cloned.1.call-start = ((), (), s32[]{:S(2)}) async-start(), calls=%async_computation.4 | async-start | bytes 262144 | tf_op jit(solution)/shard_map/psum | solution.py:86
  127.6 4.3 %copy-start.1 = (f32[192,64]{0,1:T(8,128)S(1)}, f32[192,64]{0,1:T(8,128)}, u32[]{:S(2)}) copy-start(f32[192,64]{0,1:T(8,128)} %get-tuple-element.11) | copy-start | bytes 147460
Sparse Core Ops, SparseCore 0:
  83.1 19.3 all-reduce.4
  104.8 22.7 all-reduce.6
